TPU v7x, 32 devices: a whole 2x2x4 slice. The times are simulated.
32 devices in a mesh: replica: 2 (over x), fsdp: 16 (over z, y, core).
Axes of the slice: x: 2, y: 2, z: 4, core: 2. Of those that a mesh axis runs over, the one named last changes fastest.
Arguments:
- tokens: bfloat16 [4096, 8192], P(('replica', 'fsdp')), may hold values from -400 to 400
- cotangent: bfloat16 [4096, 512], P(('replica', 'fsdp')), may hold values from -6 to 6
- gain: float32 [2, 8192], P('replica'), may hold values from 0.1 to 1.9
- local_weight: float32 [2, 8192, 512], P('replica', 'fsdp'), may hold values from -6 to 6
- stale_weight: float32 [2, 8192, 512], P('replica', 'fsdp'), may hold values from -6 to 6
- global_weight: float32 [8192, 512], P('fsdp'), may hold values from -6 to 6
- momentum: float32 [8192, 512], P('fsdp'), may hold values from -3 to 3
Outputs:
- local_new: float32 [2, 8192, 512], P('replica', 'fsdp')
- gain_new: float32 [2, 8192], P('replica')
- global_new: float32 [8192, 512], P('fsdp')
- momentum_new: float32 [8192, 512], P('fsdp')
All inputs are finite; a program needn't handle non-finite values.
Results may differ from a plain program's by a relative error of at most 0.00053.
Values may be sent and summed in bfloat16 or wider, within the bound.
A program may use at most 64 MiB of HBM per device.

v0:
```python
import jax
import jax.numpy as jnp
from jax import lax
from jax.sharding import PartitionSpec as P

HEAD = 128
KV_HEADS = 4


EPS = 1e-05
LR_INNER = 0.3
LR_GAIN = 0.01
LR_OUTER = 0.7
MOMENT = 0.9
MIXING = 0.5


def outer_step(global_weight, stale_weight, momentum):
    delta = global_weight - stale_weight[0]
    total = lax.psum(delta, "replica")
    outer_mean = total / lax.axis_size("replica")
    momentum_new = MOMENT * momentum + outer_mean
    global_new = global_weight - LR_OUTER * (outer_mean + MOMENT * momentum_new)
    return (global_new, momentum_new)


def head_backward(keys, cot32):
    rows = keys.shape[0]
    keys_h = keys.reshape(rows, KV_HEADS, HEAD)
    cot_h = cot32.reshape(rows, KV_HEADS, HEAD)
    key_scale = lax.rsqrt(jnp.mean(keys_h * keys_h, axis=2, keepdims=True) + EPS)
    unit_keys = keys_h * key_scale
    along = jnp.mean(cot_h * unit_keys, axis=2, keepdims=True)
    return (
        (key_scale * (cot_h - unit_keys * along))
        .reshape(rows, KV_HEADS * HEAD)
        .astype(jnp.bfloat16)
    )


def body(tokens, cotangent, gain, local_weight, stale_weight, global_weight, momentum):
    factor = tokens.shape[1] ** (-0.5)
    gain_row = gain[0]
    weight = local_weight[0]
    tok32 = tokens.astype(jnp.float32)
    inv_rms = lax.rsqrt(jnp.mean(tok32 * tok32, axis=1, keepdims=True) + EPS)
    scaled = tok32 * inv_rms
    normed = (scaled * gain_row[None, :]).astype(jnp.bfloat16)
    weight_bf = weight.astype(jnp.bfloat16)
    full_weight = lax.all_gather(weight_bf, "fsdp", axis=0, tiled=True)
    keys = jnp.dot(normed, full_weight, preferred_element_type=jnp.float32) * factor
    dproj = head_backward(keys, cotangent.astype(jnp.float32))
    dnormed = (
        lax.dot_general(
            dproj, full_weight, (((1,), (1,)), ((), ())), preferred_element_type=jnp.float32
        )
        * factor
    )
    gain_term = jnp.sum(scaled * dnormed, axis=0)
    gain_total = lax.psum(gain_term, "fsdp")
    moved = lax.all_to_all(normed, "fsdp", split_axis=1, concat_axis=0, tiled=True)
    all_dproj = lax.all_gather(dproj, "fsdp", axis=0, tiled=True)
    weight_grad = (
        lax.dot_general(
            moved, all_dproj, (((0,), (0,)), ((), ())), preferred_element_type=jnp.float32
        )
        * factor
    )
    global_new, momentum_new = outer_step(global_weight, stale_weight, momentum)
    inner = weight - LR_INNER * weight_grad
    local_new = MIXING * inner + (1.0 - MIXING) * global_new
    gain_new = gain_row - LR_GAIN * gain_total
    return (local_new[None], gain_new[None], global_new, momentum_new)


def solution(mesh):
    return jax.shard_map(
        body,
        mesh=mesh,
        in_specs=(
            P(("replica", "fsdp"), None),
            P(("replica", "fsdp"), None),
            P("replica", None),
            P("replica", "fsdp", None),
            P("replica", "fsdp", None),
            P("fsdp", None),
            P("fsdp", None),
        ),
        out_specs=(
            P("replica", "fsdp", None),
            P("replica", None),
            P("fsdp", None),
            P("fsdp", None),
        ),
        check_vma=False,
    )
```

profile of v0, /device:TPU:0, one launch (start us, length us, event | category | flops | bytes accessed | tf_op | source)
XLA Modules:
  0.0 215.9 jit_solution(17850435875952366364)
XLA Ops:
  8.0 0.0 copy-start.5
  8.0 0.0 all-gather.3.cloned.1.call-start
  8.1 2.1 bitcast_convert_fusion
  10.1 0.0 all-gather.3.cloned.1.call-update
  10.2 2.1 fusion.3
  12.3 0.0 copy-done.5
  12.3 2.2 %fusion.2 = bf16[128,8192]{1,0:T(8,128)(2,1)S(1)} fusion(bf16[128,8192]{1,0:T(8,128)(2,1)} %param.7, f32[8192]{0:T(1024)S(1)} %bitcast.41, f32[128]{0:T(128)S(1)} %add_rsqrt_fusion.1), kind=kLoop, calls=%fused_computation.5 | loop fusion | flops 4194304 | bytes 4227584 | tf_op jit(solution)/shard_map/convert_element_type | solution.py:48
  14.4 0.0 copy-start.1
  14.4 1.5 copy.18
  16.0 7.6 %all-to-all-start = ((bf16[128,16,512]{2,0,1:T(8,128)(2,1)}), bf16[128,16,512]{2,0,1:T(8,128)(2,1)}, u32[]{:S(2)}, u32[]{:S(2)}) async-start(bf16[128,16,512]{2,0,1:T(8,128)(2,1)} %bitcast.38), calls=%async_computation | async-start | bytes 4194304 | tf_op jit(solution)/shard_map/all_to_all | solution.py:61
  23.6 0.0 all-reduce.2.cloned.1.call-start
  23.6 2.4 %bitcast_subtract_fusion = f32[512,512]{1,0:T(8,128)} fusion(f32[512,512]{1,0:T(8,128)S(1)} %copy-done.1, f32[1,512,512]{2,1,0:T(8,128)} %param.11), kind=kLoop, calls=%fused_computation.15 | loop fusion | flops 262144 | bytes 3145728 | tf_op jit(solution)/shard_map/sub | solution.py:19
  26.0 0.0 all-reduce.2.cloned.1.call-update
  26.1 0.0 all-gather.5.cloned.1.call-start
  26.1 0.8 reshape.42
  26.9 97.3 %all-gather.3.cloned.1.call-done = bf16[8192,512]{1,0:T(8,128)(2,1)} async-done(((bf16[512,512]{1,0:T(8,128)(2,1)}), bf16[8192,512]{1,0:T(8,128)(2,1)}) %all-gather.3.cloned.1.call-update) | async-done | bytes 8388624 | tf_op jit(solution)/shard_map/all_gather | solution.py:50
  124.2 4.6 %convolution_multiply_fusion.2 = f32[128,512]{1,0:T(8,128)S(1)} fusion(bf16[128,8192]{1,0:T(8,128)(2,1)S(1)} %fusion.2, bf16[8192,512]{1,0:T(8,128)(2,1)} %all-gather.3.cloned.1.call-done), kind=kOutput, calls=%fused_computation.14 | convolution fusion | flops 1073807360 | bytes 10747904 | tf_op jit(solution)/shard_map/dot_general | solution.py:51
  128.9 0.8 reshape.41
  129.7 1.3 multiply_reduce_fusion.1
  131.0 1.4 multiply_reduce_fusion
  132.4 0.2 mul.117
  132.6 0.2 mul.112
  132.8 0.7 fusion.11
  133.6 0.0 all-gather.5.cloned.1.call-update
  133.6 0.0 all-reduce.2.cloned.1.call-done
  133.6 3.2 %multiply_subtract_fusion = (f32[512,512]{1,0:T(8,128)}, f32[512,512]{1,0:T(8,128)}) fusion(f32[512,512]{1,0:T(8,128)S(1)} %copy-done.1, f32[512,512]{1,0:T(8,128)} %all-reduce.2.cloned.1.call-done, f32[512,512]{1,0:T(8,128)} %param.13), kind=kLoop, calls=%fused_computation.17 | loop fusion | flops 1835008 | bytes 5242880 | tf_op jit(solution)/shard_map/sub | solution.py:23
  136.9 0.0 copy-start.2
  136.9 6.3 %fusion.4 = f32[8192]{0:T(1024)S(1)} fusion(bf16[128,512]{1,0:T(8,128)(2,1)S(1)} %copy-done.4, bf16[8192,512]{1,0:T(8,128)(2,1)} %all-gather.3.cloned.1.call-done, f32[128]{0:T(128)S(1)} %add_rsqrt_fusion.1, bf16[128,8192]{1,0:T(8,128)(2,1)S(1)} %copy-done), kind=kOutput, calls=%fused_computation.8 | convolution fusion | flops 1078976512 | bytes 10650112 | tf_op jit(solution)/shard_map/dot_general | solution.py:54
  143.2 59.8 %psum.15 = f32[8192]{0:T(1024)S(1)} all-reduce(f32[8192]{0:T(1024)S(1)} %fusion.4), channel_id=1, replica_groups=mesh['replica'=2,'fsdp'=16] {'fsdp'}, use_global_device_ids=true, to_apply=%region_5.0 | all-reduce | flops 8192 | bytes 65536 | tf_op jit(solution)/shard_map/psum | solution.py:60
  203.1 0.6 multiply_subtract_fusion.1
  203.7 0.0 all-to-all-done
  203.7 4.7 %fusion.8 = f32[1,512,512]{2,1,0:T(8,128)} fusion(f32[512,512]{1,0:T(8,128)S(1)} %copy-done.2, bf16[2048,512]{1,0:T(8,128)(2,1)} %bitcast.3, bf16[2048,512]{1,0:T(8,128)(2,1)} %all-gather.5.cloned.1.call-done, f32[1,512,512]{2,1,0:T(8,128)} %param.10), kind=kOutput, calls=%fused_computation.13 | convolution fusion | flops 1074790400 | bytes 7340032 | tf_op jit(solution)/shard_map/dot_general | solution.py:64
  (14 shorter events, 0.1 us)
Async XLA Ops:
  8.0 4.3 %copy-start.5 = (f32[1,8192]{1,0:T(1,128)S(1)}, f32[1,8192]{1,0:T(1,128)}, u32[]{:S(2)}) copy-start(f32[1,8192]{1,0:T(1,128)} %param.9) | copy-start | bytes 98308
  8.0 116.2 %all-gather.3.cloned.1.call-start = ((), (), s32[]{:S(2)}) async-start(), calls=%async_computation.1 | async-start | bytes 8912896 | tf_op jit(solution)/shard_map/all_gather | solution.py:50
  14.4 9.2 %copy-start.1 = (f32[512,512]{1,0:T(8,128)S(1)}, f32[512,512]{1,0:T(8,128)}, u32[]{:S(2)}) copy-start(f32[512,512]{1,0:T(8,128)} %param.12) | copy-start | bytes 3145732
  16.0 10.1 %copy-start.3 = (bf16[128,512]{1,0:T(8,128)(2,1)S(1)}, bf16[128,512]{1,0:T(8,128)(2,1)}, u32[]{:S(2)}) copy-start(bf16[128,512]{1,0:T(8,128)(2,1)} %param.8) | copy-start | bytes 393220
  16.0 187.7 %all-to-all-start = ((bf16[128,16,512]{2,0,1:T(8,128)(2,1)}), bf16[128,16,512]{2,0,1:T(8,128)(2,1)}, u32[]{:S(2)}, u32[]{:S(2)}) async-start(bf16[128,16,512]{2,0,1:T(8,128)(2,1)} %bitcast.38), calls=%async_computation | async-start | bytes 4194304 | tf_op jit(solution)/shard_map/all_to_all | solution.py:61
  23.6 110.1 %all-reduce.2.cloned.1.call-start = ((), (), s32[]{:S(2)}) async-start(), calls=%async_computation.3 | async-start | bytes 2097152 | tf_op jit(solution)/shard_map/psum | solution.py:20
  26.1 177.6 %all-gather.5.cloned.1.call-start = ((), (), s32[]{:S(2)}) async-start(), calls=%async_computation.2 | async-start | bytes 2228224 | tf_op jit(solution)/shard_map/all_gather | solution.py:62
  129.7 7.2 %copy-start = (bf16[128,8192]{1,0:T(8,128)(2,1)S(1)}, bf16[128,8192]{1,0:T(8,128)(2,1)}, u32[]{:S(2)}) copy-start(bf16[128,8192]{1,0:T(8,128)(2,1)} %param.7) | copy-start | bytes 6291460
  133.6 3.3 %copy-start.4 = (bf16[128,512]{1,0:T(8,128)(2,1)S(1)}, bf16[128,512]{1,0:T(8,128)(2,1)}, u32[]{:S(2)}) copy-start(bf16[128,512]{1,0:T(8,128)(2,1)} %fusion.11) | copy-start | bytes 393220
  136.9 66.2 %copy-start.6 = (f32[1,8192]{1,0:T(1,128)S(1)}, f32[1,8192]{1,0:T(1,128)}, u32[]{:S(2)}) copy-start(f32[1,8192]{1,0:T(1,128)} %param.9) | copy-start | bytes 98308
  136.9 66.8 %copy-start.2 = (f32[512,512]{1,0:T(8,128)S(1)}, f32[512,512]{1,0:T(8,128)}, u32[]{:S(2)}) copy-start(f32[512,512]{1,0:T(8,128)} %get-tuple-element.4) | copy-start | bytes 3145732
Sparse Core Ops, SparseCore 0:
  11.8 112.3 all-gather.2
  133.7 40.4 all-gather.4
Sparse Core Ops, SparseCore 1:
  26.9 41.1 all-reduce.1
where the time goes:
time: 216 us
  waiting for transfers between devices  97.4 us (45%)
  blocking collectives  59.8 us (28%)
  other arithmetic  16.1 us (7%)
  matrix products  15.7 us (7%)
  between operations  15.6 us (7%)
  starting transfers between devices  7.69 us (4%)
  local copies, waits for them, and re-layouts  3.54 us (2%)
    all_gather x1, waiting for transfers between devices, body(): full_weight = lax.all_gather(weight_bf, 'fsdp', axis=0, tiled=True)  97.3 us
    psum x1, blocking collectives, body(): gain_total = lax.psum(gain_term, 'fsdp')  59.8 us
    all_to_all x1, starting transfers between devices, body(): lax.all_to_all(normed, 'fsdp', split_axis=1, concat_axis=0, tiled=True)  7.57 us
    dot_general x1, matrix products, body(): lax.dot_general(dproj, full_weight, (((1,), (1,)), ((), ())), preferred_e...  6.34 us
    dot_general x1, matrix products, body(): lax.dot_general(moved, all_dproj, (((0,), (0,)), ((), ())), preferred_ele...  4.75 us
    dot_general x1, matrix products, body(): jnp.dot(normed, full_weight, preferred_element_type=jnp.float32) * factor  4.64 us
  transfers between devices with their start and end apart: 4, of which 1 were waited for; matrix products, arithmetic and copies ran while one was open for 13% of the time, Pallas kernels for 0%

commit v1 on v0

v1 whole, which is shorter than its diff:
```python
import functools

import jax
import jax.numpy as jnp
from jax import lax
from jax.experimental import pallas as pl
from jax.experimental.pallas import tpu as pltpu
from jax.sharding import PartitionSpec as P

HEAD = 128
KV_HEADS = 4


EPS = 1e-05
LR_INNER = 0.3
LR_GAIN = 0.01
LR_OUTER = 0.7
MOMENT = 0.9
MIXING = 0.5

MESH = pl.DeviceIdType.MESH
PLANE = 4


def head_backward(keys, cot32):
    parts = []
    for h in range(KV_HEADS):
        cols = slice(h * HEAD, (h + 1) * HEAD)
        keys_h = keys[:, cols]
        cot_h = cot32[:, cols]
        key_scale = lax.rsqrt(jnp.mean(keys_h * keys_h, axis=1, keepdims=True) + EPS)
        unit_keys = keys_h * key_scale
        along = jnp.mean(cot_h * unit_keys, axis=1, keepdims=True)
        parts.append((key_scale * (cot_h - unit_keys * along)).astype(jnp.bfloat16))
    return jnp.concatenate(parts, axis=1)


def kernel(
    n, n_rep, factor,
    tok_ref, cot_ref, gain_ref, weight_ref, stale_ref, global_ref, mom_ref,
    local_out, gain_out, global_out, mom_out,
    normed_buf, x_all, w_bf, part_f32, part_bf, plane_recv, keys_send, keys_recv,
    keys_acc, dproj_all, grad_acc, delta_buf, delta_recv, gain_buf,
    x_send_sem, x_recv_sem, plane_send_sem, plane_recv_sem, keys_send_sem,
    keys_recv_sem, dproj_send_sem, dproj_recv_sem, delta_send_sem, delta_recv_sem,
    gain_send_sem, gain_recv_sem,
):
    rep = lax.axis_index("replica")
    me = lax.axis_index("fsdp")
    planes = n // PLANE
    z, q = me // PLANE, me % PLANE
    rows = tok_ref.shape[0]
    feats = weight_ref.shape[0]

    def at(plane, place):
        return plane * PLANE + place

    def turned(d):
        return lax.rem(z + d, planes)

    def send(src, dst, send_sem, recv_sem, target, replica=None):
        pltpu.make_async_remote_copy(
            src_ref=src, dst_ref=dst, send_sem=send_sem, recv_sem=recv_sem,
            device_id=(rep if replica is None else replica, target), device_id_type=MESH,
        ).start()

    def wait_bytes(ref, sem):
        pltpu.make_async_copy(ref, ref, sem).wait()

    barrier = pltpu.get_barrier_semaphore()
    for i in range(1, n):
        pl.semaphore_signal(
            barrier, inc=1, device_id=(rep, lax.rem(me + i, n)), device_id_type=MESH
        )
    for i in range(1, n_rep):
        pl.semaphore_signal(
            barrier, inc=1, device_id=(lax.rem(rep + i, n_rep), me), device_id_type=MESH
        )

    total = jnp.zeros((rows, 1), jnp.float32)
    for j in range(n):
        piece = tok_ref[:, j * feats:(j + 1) * feats].astype(jnp.float32)
        total += jnp.sum(piece * piece, axis=1, keepdims=True)
    inv_rms = lax.rsqrt(total / tok_ref.shape[1] + EPS)
    for j in range(n):
        cols = slice(j * feats, (j + 1) * feats)
        scaled = tok_ref[:, cols].astype(jnp.float32) * inv_rms
        normed_buf[j] = (scaled * gain_ref[:, cols]).astype(jnp.bfloat16)
    pl.semaphore_wait(barrier, n - 1 + n_rep - 1)

    def block_rows(index):
        return pl.ds(pl.multiple_of(index * rows, rows), rows)

    def plane_rows(plane):
        return pl.ds(pl.multiple_of(plane * (PLANE * rows), PLANE * rows), PLANE * rows)

    for d in range(planes):
        for e in range(PLANE):
            if d == 0 and e == 0:
                continue
            target = at(turned(d), lax.rem(q + e, PLANE))
            send(normed_buf.at[target], x_all.at[block_rows(me), :], x_send_sem,
                 x_recv_sem.at[z], target)
    delta_buf[...] = global_ref[...] - stale_ref[...]
    for i in range(1, n_rep):
        send(delta_buf, delta_recv.at[i - 1], delta_send_sem, delta_recv_sem, me,
             lax.rem(rep + i, n_rep))
    x_all[block_rows(me), :] = normed_buf[me]
    w_bf[...] = weight_ref[...].astype(jnp.bfloat16)

    def partial_keys(d):
        plane = turned(planes - d)
        count = PLANE - 1 if d == 0 else PLANE
        wait_bytes(x_all.at[pl.ds(0, count * rows), :], x_recv_sem.at[plane])
        part = jnp.dot(x_all[plane_rows(plane), :], w_bf[...],
                       preferred_element_type=jnp.float32)
        part_f32[d] = part
        part_bf[d] = part.astype(jnp.bfloat16)
        for e in range(1, PLANE):
            place = lax.rem(q + e, PLANE)
            send(part_bf.at[d, block_rows(place), :], plane_recv.at[d, e - 1],
                 plane_send_sem, plane_recv_sem.at[d], at(z, place))

    def plane_sum(d):
        wait_bytes(plane_recv.at[d], plane_recv_sem.at[d])
        summed = part_f32[d, block_rows(q), :]
        for e in range(PLANE - 1):
            summed += plane_recv[d, e].astype(jnp.float32)
        if d == 0:
            keys_acc[...] = summed
        else:
            keys_send[d - 1] = summed.astype(jnp.bfloat16)
            send(keys_send.at[d - 1], keys_recv.at[d - 1], keys_send_sem,
                 keys_recv_sem, at(turned(planes - d), q))

    partial_keys(0)
    for d in range(1, planes):
        partial_keys(d)
        plane_sum(d - 1)
    plane_sum(planes - 1)

    wait_bytes(delta_recv, delta_recv_sem)
    outer = delta_buf[...]
    for i in range(n_rep - 1):
        outer += delta_recv[i]
    outer_mean = outer / n_rep
    momentum_new = MOMENT * mom_ref[...] + outer_mean
    global_new = global_ref[...] - LR_OUTER * (outer_mean + MOMENT * momentum_new)
    mom_out[...] = momentum_new
    global_out[...] = global_new
    local_out[...] = MIXING * weight_ref[...] + (1.0 - MIXING) * global_new

    wait_bytes(keys_recv, keys_recv_sem)
    keys = keys_acc[...]
    for d in range(planes - 1):
        keys += keys_recv[d].astype(jnp.float32)
    dproj_all[block_rows(me), :] = head_backward(
        keys * factor, cot_ref[...].astype(jnp.float32)
    )

    pair = lax.rem(q + 2, PLANE)
    core = q + 1 - 2 * lax.rem(q, 2)
    last = lax.rem(core + 2, PLANE)

    def pass_on(index, target):
        block = dproj_all.at[block_rows(index), :]
        send(block, block, dproj_send_sem, dproj_recv_sem.at[index], target)

    def arrived(index):
        wait_bytes(dproj_all.at[block_rows(index), :], dproj_recv_sem.at[index])

    for d in range(1, planes):
        pass_on(me, at(turned(d), q))
    pass_on(me, at(z, pair))
    pass_on(me, at(z, core))

    def from_plane(d):
        index = at(turned(planes - d), q)
        arrived(index)
        pass_on(index, at(z, pair))
        pass_on(index, at(z, core))

    def from_pair(d):
        index = at(turned(planes - d), pair)
        arrived(index)
        pass_on(index, at(z, core))

    def add_plane(d):
        plane = turned(planes - d)
        arrived(at(plane, core))
        arrived(at(plane, last))
        product = lax.dot_general(
            x_all[plane_rows(plane), :], dproj_all[plane_rows(plane), :],
            (((0,), (0,)), ((), ())), preferred_element_type=jnp.float32,
        )
        if d == 0:
            grad_acc[...] = product
        else:
            grad_acc[...] += product

    for d in range(1, planes + 2):
        if d < planes:
            from_plane(d)
        if d - 1 < planes:
            from_pair(d - 1)
        if d >= 2:
            add_plane(d - 2)

    grad = grad_acc[...] * factor
    ones = jnp.ones((8, grad.shape[1]), jnp.float32)
    row = lax.dot_general(
        ones, w_bf[...].astype(jnp.float32) * grad, (((1,), (1,)), ((), ())),
        precision=lax.Precision.HIGHEST, preferred_element_type=jnp.float32,
    )[0:1, :]
    gain_own = gain_ref[:, pl.ds(pl.multiple_of(me * feats, feats), feats)]
    gain_buf[me] = gain_own - LR_GAIN * (row / gain_own)
    for i in range(1, n):
        send(gain_buf.at[me], gain_buf.at[me], gain_send_sem, gain_recv_sem,
             lax.rem(me + i, n))
    local_out[...] -= MIXING * LR_INNER * grad

    wait_bytes(normed_buf.at[pl.ds(0, n - 1)], x_send_sem)
    wait_bytes(plane_recv, plane_send_sem)
    wait_bytes(keys_send, keys_send_sem)
    wait_bytes(dproj_all.at[pl.ds(0, (n - 1) * rows), :], dproj_send_sem)
    wait_bytes(delta_recv, delta_send_sem)
    wait_bytes(gain_buf.at[pl.ds(0, n - 1)], gain_recv_sem)
    for j in range(n):
        gain_out[:, j * feats:(j + 1) * feats] = gain_buf[j]
    wait_bytes(gain_buf.at[pl.ds(0, n - 1)], gain_send_sem)


def body(tokens, cotangent, gain, local_weight, stale_weight, global_weight, momentum):
    n = lax.axis_size("fsdp")
    n_rep = lax.axis_size("replica")
    rows, width = tokens.shape
    feats, units = global_weight.shape
    planes = n // PLANE
    factor = width ** (-0.5)
    f32, bf16 = jnp.float32, jnp.bfloat16
    vmem = pl.BlockSpec(memory_space=pltpu.VMEM)
    dma = pltpu.SemaphoreType.DMA
    local_new, gain_new, global_new, momentum_new = pl.pallas_call(
        functools.partial(kernel, n, n_rep, factor),
        out_shape=(
            jax.ShapeDtypeStruct((feats, units), f32),
            jax.ShapeDtypeStruct((1, width), f32),
            jax.ShapeDtypeStruct((feats, units), f32),
            jax.ShapeDtypeStruct((feats, units), f32),
        ),
        in_specs=[vmem] * 7,
        out_specs=(vmem,) * 4,
        scratch_shapes=[
            pltpu.VMEM((n, rows, feats), bf16),
            pltpu.VMEM((n * rows, feats), bf16),
            pltpu.VMEM((feats, units), bf16),
            pltpu.VMEM((planes, PLANE * rows, units), f32),
            pltpu.VMEM((planes, PLANE * rows, units), bf16),
            pltpu.VMEM((planes, PLANE - 1, rows, units), bf16),
            pltpu.VMEM((planes - 1, rows, units), bf16),
            pltpu.VMEM((planes - 1, rows, units), bf16),
            pltpu.VMEM((rows, units), f32),
            pltpu.VMEM((n * rows, units), bf16),
            pltpu.VMEM((feats, units), f32),
            pltpu.VMEM((feats, units), f32),
            pltpu.VMEM((n_rep - 1, feats, units), f32),
            pltpu.VMEM((n, 1, feats), f32),
            dma, dma((planes,)),
            dma, dma((planes,)),
            dma, dma,
            dma, dma((n,)),
            dma, dma,
            dma, dma,
        ],
        compiler_params=pltpu.CompilerParams(
            collective_id=0, has_side_effects=True, vmem_limit_bytes=58 * 1024 * 1024
        ),
        name="diloco_step",
    )(
        tokens, cotangent, gain, local_weight[0], stale_weight[0], global_weight, momentum
    )
    return (local_new[None], gain_new, global_new, momentum_new)


def solution(mesh):
    return jax.shard_map(
        body,
        mesh=mesh,
        in_specs=(
            P(("replica", "fsdp"), None),
            P(("replica", "fsdp"), None),
            P("replica", None),
            P("replica", "fsdp", None),
            P("replica", "fsdp", None),
            P("fsdp", None),
            P("fsdp", None),
        ),
        out_specs=(
            P("replica", "fsdp", None),
            P("replica", None),
            P("fsdp", None),
            P("fsdp", None),
        ),
        check_vma=False,
    )
```

time: 216 us -> 109 us (0.50)
  Pallas kernels: 0 us -> 103 us
  waiting for transfers between devices: 97.4 us -> 0 us
  blocking collectives: 59.8 us -> 0 us
  other arithmetic: 16.1 us -> 0 us
  matrix products: 15.7 us -> 0 us
  between operations: 15.6 us -> 0.67 us
  starting transfers between devices: 7.69 us -> 0 us
    pallas_call x0 -> x1, Pallas kernels: none -> 103 us  [body(): pl.pallas_call(functools.partial(kernel, n, n_rep, factor), out_shape=(ja...]
    all_gather x2 -> x0, waiting for transfers between devices: 97.3 us -> none  [the longest x1 97.3 us: body(): full_weight = lax.all_gather(weight_bf, 'fsdp', axis=0, tiled=True)]
    psum x1 -> x0, blocking collectives: 59.8 us -> none  [body(): gain_total = lax.psum(gain_term, 'fsdp')]
    dot_general x3 -> x0, matrix products: 15.7 us -> none  [the longest x1 6.34 us: body(): lax.dot_general(dproj, full_weight, (((1,), (1,)), ((), ())), preferred_e...]
    all_to_all x1 -> x0, starting transfers between devices: 7.57 us -> none  [body(): lax.all_to_all(normed, 'fsdp', split_axis=1, concat_axis=0, tiled=True)]
    sub x3 -> x0, other arithmetic: 6.27 us -> none  [the longest x1 3.25 us: outer_step(): global_new = global_weight - LR_OUTER * (outer_mean + MOMENT * momentum_new)]
    convert_element_type x3 -> x0, other arithmetic: 4.98 us -> none  [the longest x1 2.17 us: body(): normed = (scaled * gain_row[None, :]).astype(jnp.bfloat16)]
    unnamed x14 -> x10, local copies, waits for them, and re-layouts: 0.03 us -> 4.98 us
  transfers between devices with their start and end apart: 4 -> 0, of which waited for: 1 -> 0; matrix products, arithmetic and copies ran while one was open for 13% -> 0% of each run, Pallas kernels for 0% -> 0%
where the time goes in v1:
time: 109 us; the launch traced here: 108 us
  Pallas kernels  103 us (94%)
  local copies, waits for them, and re-layouts  4.98 us (5%)
    pallas_call x1, Pallas kernels, body(): pl.pallas_call(functools.partial(kernel, n, n_rep, factor), out_shape=(ja...  103 us
    unnamed x10, local copies, waits for them, and re-layouts  4.98 us

profile of v1, /device:TPU:0, one launch (start us, length us, event | category | flops | bytes accessed | tf_op | source)
XLA Modules:
  0.0 108.4 jit_solution(15991391957564810196)
XLA Ops:
  0.6 102.8 %diloco_step.1 = (f32[512,512]{1,0:T(8,128)}, f32[1,8192]{1,0:T(1,128)}, f32[512,512]{1,0:T(8,128)}, f32[512,512]{1,0:T(8,128)}) custom-call(bf16[128,8192]{1,0:T(8,128)(2,1)} %tok_ref.1, bf16[128,512]{1,0:T(8,128)(2,1)} %cot_ref.1, f32[1,8192]{1,0:T(1,128)} %gain_ref.1, f32[512,512]{1,0:T(8,128)} %bitcast.3, f32[512,512]{1,0:T(8,128)} %bitcast.4, ...), custom_call_target="tpu_custom_call" | custom-call | tf_op jit(solution)/shard_map/diloco_step/pallas_call | solution.py:243
  103.4 0.0 copy-start.2
  103.4 0.0 copy-start.1
  103.5 0.0 copy-start
  103.5 2.4 %copy.15 = f32[1,512,512]{2,1,0:T(8,128)} copy(f32[1,512,512]{2,1,0:T(8,128)} %bitcast.5) | data formatting | bytes 2097152
  105.9 0.0 copy-done.2
  105.9 0.6 copy.16
  106.5 0.0 copy-done.1
  106.5 1.0 copy.17
  107.5 0.0 copy-done
  107.5 1.0 copy.18
Async XLA Ops:
  103.4 2.4 %copy-start.2 = (f32[1,8192]{1,0:T(1,128)S(1)}, f32[1,8192]{1,0:T(1,128)}, u32[]{:S(2)}) copy-start(f32[1,8192]{1,0:T(1,128)} %get-tuple-element.17) | copy-start | bytes 98308
  103.4 3.1 %copy-start.1 = (f32[512,512]{1,0:T(8,128)S(1)}, f32[512,512]{1,0:T(8,128)}, u32[]{:S(2)}) copy-start(f32[512,512]{1,0:T(8,128)} %get-tuple-element.18) | copy-start | bytes 3145732
  103.5 4.0 %copy-start = (f32[512,512]{1,0:T(8,128)S(1)}, f32[512,512]{1,0:T(8,128)}, u32[]{:S(2)}) copy-start(f32[512,512]{1,0:T(8,128)} %get-tuple-element.19) | copy-start | bytes 3145732

commit v2 on v1

--- a/solution.py
+++ b/solution.py
@@ -37,26 +37,38 @@
 
 def kernel(
     n, n_rep, factor,
-    tok_ref, cot_ref, gain_ref, weight_ref, stale_ref, global_ref, mom_ref,
-    local_out, gain_out, global_out, mom_out,
-    normed_buf, x_all, w_bf, part_f32, part_bf, plane_recv, keys_send, keys_recv,
+    tok_ref, cot_ref, gain_ref, weight_hbm, stale_hbm, global_hbm,
+    grad_out, gain_out, outer_out,
+    weight_ref, stale_ref, global_ref,
+    normed_buf, x_all, w_bf, part_f32, part_bf, core_recv, pair_send, pair_recv, keys_send, keys_recv,
     keys_acc, dproj_all, grad_acc, delta_buf, delta_recv, gain_buf,
-    x_send_sem, x_recv_sem, plane_send_sem, plane_recv_sem, keys_send_sem,
+    x_send_sem, x_recv_sem, core_send_sem, core_recv_sem, pair_send_sem, pair_recv_sem, keys_send_sem,
     keys_recv_sem, dproj_send_sem, dproj_recv_sem, delta_send_sem, delta_recv_sem,
-    gain_send_sem, gain_recv_sem,
+    gain_send_sem, gain_recv_sem, load_sem,
 ):
     rep = lax.axis_index("replica")
     me = lax.axis_index("fsdp")
     planes = n // PLANE
     z, q = me // PLANE, me % PLANE
+    pair = lax.rem(q + 2, PLANE)
+    core = q + 1 - 2 * lax.rem(q, 2)
+    last = lax.rem(core + 2, PLANE)
     rows = tok_ref.shape[0]
-    feats = weight_ref.shape[0]
+    feats = weight_hbm.shape[0]
 
     def at(plane, place):
         return plane * PLANE + place
 
-    def turned(d):
-        return lax.rem(z + d, planes)
+    def across(m):
+        plane, bit = z, 1
+        while bit < planes:
+            if m & bit:
+                plane = plane + bit - 2 * bit * lax.rem(z // bit, 2)
+            bit *= 2
+        return plane
+
+    half = planes // 2
+    order = [*range(half, planes), *range(1, half)]
 
     def send(src, dst, send_sem, recv_sem, target, replica=None):
         pltpu.make_async_remote_copy(
@@ -77,15 +89,26 @@
             barrier, inc=1, device_id=(lax.rem(rep + i, n_rep), me), device_id_type=MESH
         )
 
+    loads = [
+        pltpu.make_async_copy(src, dst, load_sem.at[i])
+        for i, (src, dst) in enumerate(
+            ((weight_hbm, weight_ref), (stale_hbm, stale_ref), (global_hbm, global_ref))
+        )
+    ]
+    for load in loads:
+        load.start()
+
     total = jnp.zeros((rows, 1), jnp.float32)
     for j in range(n):
         piece = tok_ref[:, j * feats:(j + 1) * feats].astype(jnp.float32)
         total += jnp.sum(piece * piece, axis=1, keepdims=True)
     inv_rms = lax.rsqrt(total / tok_ref.shape[1] + EPS)
-    for j in range(n):
-        cols = slice(j * feats, (j + 1) * feats)
+
+    def normalize(index):
+        cols = pl.ds(pl.multiple_of(index * feats, feats), feats)
         scaled = tok_ref[:, cols].astype(jnp.float32) * inv_rms
-        normed_buf[j] = (scaled * gain_ref[:, cols]).astype(jnp.bfloat16)
+        return (scaled * gain_ref[:, cols]).astype(jnp.bfloat16)
+
     pl.semaphore_wait(barrier, n - 1 + n_rep - 1)
 
     def block_rows(index):
@@ -94,61 +117,68 @@
     def plane_rows(plane):
         return pl.ds(pl.multiple_of(plane * (PLANE * rows), PLANE * rows), PLANE * rows)
 
-    for d in range(planes):
+    for d in [*order, 0]:
         for e in range(PLANE):
             if d == 0 and e == 0:
                 continue
-            target = at(turned(d), lax.rem(q + e, PLANE))
+            target = at(across(d), lax.rem(q + e, PLANE))
+            normed_buf[target] = normalize(target)
             send(normed_buf.at[target], x_all.at[block_rows(me), :], x_send_sem,
                  x_recv_sem.at[z], target)
+    for load in loads:
+        load.wait()
     delta_buf[...] = global_ref[...] - stale_ref[...]
     for i in range(1, n_rep):
         send(delta_buf, delta_recv.at[i - 1], delta_send_sem, delta_recv_sem, me,
              lax.rem(rep + i, n_rep))
-    x_all[block_rows(me), :] = normed_buf[me]
+    x_all[block_rows(me), :] = normalize(me)
     w_bf[...] = weight_ref[...].astype(jnp.bfloat16)
 
     def partial_keys(d):
-        plane = turned(planes - d)
+        plane = across(d)
         count = PLANE - 1 if d == 0 else PLANE
         wait_bytes(x_all.at[pl.ds(0, count * rows), :], x_recv_sem.at[plane])
         part = jnp.dot(x_all[plane_rows(plane), :], w_bf[...],
                        preferred_element_type=jnp.float32)
         part_f32[d] = part
         part_bf[d] = part.astype(jnp.bfloat16)
-        for e in range(1, PLANE):
-            place = lax.rem(q + e, PLANE)
-            send(part_bf.at[d, block_rows(place), :], plane_recv.at[d, e - 1],
-                 plane_send_sem, plane_recv_sem.at[d], at(z, place))
+        for e, place in enumerate((last, core)):
+            send(part_bf.at[d, block_rows(place), :], core_recv.at[d, e],
+                 core_send_sem, core_recv_sem.at[d], at(z, core))
+
+    def core_sum(d):
+        wait_bytes(core_recv.at[d], core_recv_sem.at[d])
+        pair_send[d] = (
+            part_f32[d, block_rows(pair), :] + core_recv[d, 0].astype(jnp.float32)
+        ).astype(jnp.bfloat16)
+        send(pair_send.at[d], pair_recv.at[d], pair_send_sem, pair_recv_sem.at[d],
+             at(z, pair))
 
     def plane_sum(d):
-        wait_bytes(plane_recv.at[d], plane_recv_sem.at[d])
-        summed = part_f32[d, block_rows(q), :]
-        for e in range(PLANE - 1):
-            summed += plane_recv[d, e].astype(jnp.float32)
+        summed = part_f32[d, block_rows(q), :] + core_recv[d, 1].astype(jnp.float32)
+        wait_bytes(pair_recv.at[d], pair_recv_sem.at[d])
+        summed += pair_recv[d].astype(jnp.float32)
         if d == 0:
             keys_acc[...] = summed
         else:
             keys_send[d - 1] = summed.astype(jnp.bfloat16)
             send(keys_send.at[d - 1], keys_recv.at[d - 1], keys_send_sem,
-                 keys_recv_sem, at(turned(planes - d), q))
-
-    partial_keys(0)
-    for d in range(1, planes):
-        partial_keys(d)
-        plane_sum(d - 1)
-    plane_sum(planes - 1)
+                 keys_recv_sem, at(across(d), q))
+
+    turns = [0, *order]
+    for step in range(planes + 2):
+        if step < planes:
+            partial_keys(turns[step])
+        if 1 <= step <= planes:
+            core_sum(turns[step - 1])
+        if step >= 2:
+            plane_sum(turns[step - 2])
 
     wait_bytes(delta_recv, delta_recv_sem)
     outer = delta_buf[...]
     for i in range(n_rep - 1):
         outer += delta_recv[i]
-    outer_mean = outer / n_rep
-    momentum_new = MOMENT * mom_ref[...] + outer_mean
-    global_new = global_ref[...] - LR_OUTER * (outer_mean + MOMENT * momentum_new)
-    mom_out[...] = momentum_new
-    global_out[...] = global_new
-    local_out[...] = MIXING * weight_ref[...] + (1.0 - MIXING) * global_new
+    outer_out[...] = outer
 
     wait_bytes(keys_recv, keys_recv_sem)
     keys = keys_acc[...]
@@ -158,9 +188,6 @@
         keys * factor, cot_ref[...].astype(jnp.float32)
     )
 
-    pair = lax.rem(q + 2, PLANE)
-    core = q + 1 - 2 * lax.rem(q, 2)
-    last = lax.rem(core + 2, PLANE)
 
     def pass_on(index, target):
         block = dproj_all.at[block_rows(index), :]
@@ -170,23 +197,23 @@
         wait_bytes(dproj_all.at[block_rows(index), :], dproj_recv_sem.at[index])
 
     for d in range(1, planes):
-        pass_on(me, at(turned(d), q))
+        pass_on(me, at(across(d), q))
     pass_on(me, at(z, pair))
     pass_on(me, at(z, core))
 
     def from_plane(d):
-        index = at(turned(planes - d), q)
+        index = at(across(d), q)
         arrived(index)
         pass_on(index, at(z, pair))
         pass_on(index, at(z, core))
 
     def from_pair(d):
-        index = at(turned(planes - d), pair)
+        index = at(across(d), pair)
         arrived(index)
         pass_on(index, at(z, core))
 
     def add_plane(d):
-        plane = turned(planes - d)
+        plane = across(d)
         arrived(at(plane, core))
         arrived(at(plane, last))
         product = lax.dot_general(
@@ -217,10 +244,11 @@
     for i in range(1, n):
         send(gain_buf.at[me], gain_buf.at[me], gain_send_sem, gain_recv_sem,
              lax.rem(me + i, n))
-    local_out[...] -= MIXING * LR_INNER * grad
+    grad_out[...] = grad
 
     wait_bytes(normed_buf.at[pl.ds(0, n - 1)], x_send_sem)
-    wait_bytes(plane_recv, plane_send_sem)
+    wait_bytes(core_recv, core_send_sem)
+    wait_bytes(pair_recv, pair_send_sem)
     wait_bytes(keys_send, keys_send_sem)
     wait_bytes(dproj_all.at[pl.ds(0, (n - 1) * rows), :], dproj_send_sem)
     wait_bytes(delta_recv, delta_send_sem)
@@ -240,23 +268,28 @@
     f32, bf16 = jnp.float32, jnp.bfloat16
     vmem = pl.BlockSpec(memory_space=pltpu.VMEM)
     dma = pltpu.SemaphoreType.DMA
-    local_new, gain_new, global_new, momentum_new = pl.pallas_call(
+    weight = local_weight[0]
+    weight_grad, gain_new, outer = pl.pallas_call(
         functools.partial(kernel, n, n_rep, factor),
         out_shape=(
             jax.ShapeDtypeStruct((feats, units), f32),
             jax.ShapeDtypeStruct((1, width), f32),
             jax.ShapeDtypeStruct((feats, units), f32),
-            jax.ShapeDtypeStruct((feats, units), f32),
         ),
-        in_specs=[vmem] * 7,
-        out_specs=(vmem,) * 4,
+        in_specs=[vmem] * 3 + [pl.BlockSpec(memory_space=pl.ANY)] * 3,
+        out_specs=(vmem,) * 3,
         scratch_shapes=[
+            pltpu.VMEM((feats, units), f32),
+            pltpu.VMEM((feats, units), f32),
+            pltpu.VMEM((feats, units), f32),
             pltpu.VMEM((n, rows, feats), bf16),
             pltpu.VMEM((n * rows, feats), bf16),
             pltpu.VMEM((feats, units), bf16),
             pltpu.VMEM((planes, PLANE * rows, units), f32),
             pltpu.VMEM((planes, PLANE * rows, units), bf16),
-            pltpu.VMEM((planes, PLANE - 1, rows, units), bf16),
+            pltpu.VMEM((planes, 2, rows, units), bf16),
+            pltpu.VMEM((planes, rows, units), bf16),
+            pltpu.VMEM((planes, rows, units), bf16),
             pltpu.VMEM((planes - 1, rows, units), bf16),
             pltpu.VMEM((planes - 1, rows, units), bf16),
             pltpu.VMEM((rows, units), f32),
@@ -265,20 +298,25 @@
             pltpu.VMEM((feats, units), f32),
             pltpu.VMEM((n_rep - 1, feats, units), f32),
             pltpu.VMEM((n, 1, feats), f32),
+            dma, dma((planes,)),
             dma, dma((planes,)),
             dma, dma((planes,)),
             dma, dma,
             dma, dma((n,)),
             dma, dma,
             dma, dma,
+            dma((3,)),
         ],
         compiler_params=pltpu.CompilerParams(
             collective_id=0, has_side_effects=True, vmem_limit_bytes=58 * 1024 * 1024
         ),
         name="diloco_step",
-    )(
-        tokens, cotangent, gain, local_weight[0], stale_weight[0], global_weight, momentum
-    )
+    )(tokens, cotangent, gain, weight, stale_weight[0], global_weight)
+    outer_mean = outer / n_rep
+    momentum_new = MOMENT * momentum + outer_mean
+    global_new = global_weight - LR_OUTER * (outer_mean + MOMENT * momentum_new)
+    inner = weight - LR_INNER * weight_grad
+    local_new = MIXING * inner + (1.0 - MIXING) * global_new
     return (local_new[None], gain_new, global_new, momentum_new)
 
 

time: 109 us -> 105 us (0.963)
  local copies, waits for them, and re-layouts: 4.98 us -> 0.63 us
  other arithmetic: 0 us -> 3.63 us
  Pallas kernels: 103 us -> 99.5 us
    unnamed x10 -> x9, local copies, waits for them, and re-layouts: 4.98 us -> 0.63 us
    broadcast_in_dim x0 -> x1, other arithmetic: none -> 3.63 us  [body(): return (local_new[None], gain_new, global_new, momentum_new)]
    pallas_call x1, Pallas kernels: 103 us -> 99.5 us  [body(): pl.pallas_call(functools.partial(kernel, n, n_rep, factor), out_shape=(ja...]
where the time goes in v2:
time: 105 us; the launch traced here: 104 us
  Pallas kernels  99.5 us (95%)
  other arithmetic  3.63 us (3%)
    pallas_call x1, Pallas kernels, body(): pl.pallas_call(functools.partial(kernel, n, n_rep, factor), out_shape=(ja...  99.5 us
    broadcast_in_dim x1, other arithmetic, body(): return (local_new[None], gain_new, global_new, momentum_new)  3.63 us

profile of v2, /device:TPU:0, one launch (start us, length us, event | category | flops | bytes accessed | tf_op | source)
XLA Modules:
  0.0 104.5 jit_solution(4340048135953129913)
XLA Ops:
  0.6 0.0 copy-start
  0.6 0.0 copy-start.1
  0.7 0.0 copy-start.2
  0.7 99.5 %diloco_step.1 = (f32[512,512]{1,0:T(8,128)}, f32[1,8192]{1,0:T(1,128)}, f32[512,512]{1,0:T(8,128)}) custom-call(bf16[128,8192]{1,0:T(8,128)(2,1)} %tok_ref.1, bf16[128,512]{1,0:T(8,128)(2,1)} %cot_ref.1, f32[1,8192]{1,0:T(1,128)} %gain_ref.1, f32[512,512]{1,0:T(8,128)} %bitcast.5, f32[512,512]{1,0:T(8,128)} %bitcast.6, f32[512,512]{1,0:T(8,128)} %global_hbm.1), custom_call_target="tpu_custom_call" | custom-call | tf_op jit(solution)/shard_map/diloco_step/pallas_call | solution.py:272
  100.2 0.0 copy-done
  100.2 0.0 copy-done.1
  100.2 0.0 copy-done.2
  100.2 0.0 copy-start.3
  100.2 3.6 %multiply_bitcast_fusion = (f32[1,512,512]{2,1,0:T(8,128)}, f32[512,512]{1,0:T(8,128)}, f32[512,512]{1,0:T(8,128)}) fusion(f32[512,512]{1,0:T(8,128)} %get-tuple-element.7, f32[1,512,512]{2,1,0:T(8,128)S(1)} %copy-done, f32[512,512]{1,0:T(8,128)S(1)} %copy-done.1, f32[512,512]{1,0:T(8,128)} %get-tuple-element.8, f32[512,512]{1,0:T(8,128)S(1)} %copy-done.2), kind=kLoop, calls=%fused_computation | loop fusion | flops 2883584 | bytes 8388608 | tf_op jit(solution)/shard_map/broadcast_in_dim | solution.py:320
  103.9 0.0 copy-done.3
  103.9 0.6 copy.12
Async XLA Ops:
  0.6 99.6 %copy-start = (f32[1,512,512]{2,1,0:T(8,128)S(1)}, f32[1,512,512]{2,1,0:T(8,128)}, u32[]{:S(2)}) copy-start(f32[1,512,512]{2,1,0:T(8,128)} %param.10) | copy-start | bytes 3145732
  0.6 99.6 %copy-start.1 = (f32[512,512]{1,0:T(8,128)S(1)}, f32[512,512]{1,0:T(8,128)}, u32[]{:S(2)}) copy-start(f32[512,512]{1,0:T(8,128)} %global_hbm.1) | copy-start | bytes 3145732
  0.7 99.6 %copy-start.2 = (f32[512,512]{1,0:T(8,128)S(1)}, f32[512,512]{1,0:T(8,128)}, u32[]{:S(2)}) copy-start(f32[512,512]{1,0:T(8,128)} %param.13) | copy-start | bytes 3145732
  100.2 3.6 %copy-start.3 = (f32[1,8192]{1,0:T(1,128)S(1)}, f32[1,8192]{1,0:T(1,128)}, u32[]{:S(2)}) copy-start(f32[1,8192]{1,0:T(1,128)} %get-tuple-element.18) | copy-start | bytes 98308

commit v3 on v2

--- a/solution.py
+++ b/solution.py
@@ -20,6 +20,7 @@
 
 MESH = pl.DeviceIdType.MESH
 PLANE = 4
+HALVES = 2
 
 
 def head_backward(keys, cot32):
@@ -53,7 +54,7 @@
     pair = lax.rem(q + 2, PLANE)
     core = q + 1 - 2 * lax.rem(q, 2)
     last = lax.rem(core + 2, PLANE)
-    rows = tok_ref.shape[0]
+    rows = tok_ref.shape[0] // HALVES
     feats = weight_hbm.shape[0]
 
     def at(plane, place):
@@ -98,15 +99,16 @@
     for load in loads:
         load.start()
 
-    total = jnp.zeros((rows, 1), jnp.float32)
+    total = jnp.zeros((rows * HALVES, 1), jnp.float32)
     for j in range(n):
         piece = tok_ref[:, j * feats:(j + 1) * feats].astype(jnp.float32)
         total += jnp.sum(piece * piece, axis=1, keepdims=True)
     inv_rms = lax.rsqrt(total / tok_ref.shape[1] + EPS)
 
-    def normalize(index):
+    def normalize(index, h):
         cols = pl.ds(pl.multiple_of(index * feats, feats), feats)
-        scaled = tok_ref[:, cols].astype(jnp.float32) * inv_rms
+        here = slice(h * rows, (h + 1) * rows)
+        scaled = tok_ref[here, cols].astype(jnp.float32) * inv_rms[here]
         return (scaled * gain_ref[:, cols]).astype(jnp.bfloat16)
 
     pl.semaphore_wait(barrier, n - 1 + n_rep - 1)
@@ -117,121 +119,138 @@
     def plane_rows(plane):
         return pl.ds(pl.multiple_of(plane * (PLANE * rows), PLANE * rows), PLANE * rows)
 
-    for d in [*order, 0]:
-        for e in range(PLANE):
-            if d == 0 and e == 0:
-                continue
-            target = at(across(d), lax.rem(q + e, PLANE))
-            normed_buf[target] = normalize(target)
-            send(normed_buf.at[target], x_all.at[block_rows(me), :], x_send_sem,
-                 x_recv_sem.at[z], target)
+    for h in range(HALVES):
+        for d in [*order, 0]:
+            for e in range(PLANE):
+                if d == 0 and e == 0:
+                    continue
+                target = at(across(d), lax.rem(q + e, PLANE))
+                normed_buf[h, target] = normalize(target, h)
+                send(normed_buf.at[h, target], x_all.at[h, block_rows(me), :],
+                     x_send_sem.at[h], x_recv_sem.at[h, z], target)
     for load in loads:
         load.wait()
     delta_buf[...] = global_ref[...] - stale_ref[...]
     for i in range(1, n_rep):
         send(delta_buf, delta_recv.at[i - 1], delta_send_sem, delta_recv_sem, me,
              lax.rem(rep + i, n_rep))
-    x_all[block_rows(me), :] = normalize(me)
+    for h in range(HALVES):
+        x_all[h, block_rows(me), :] = normalize(me, h)
     w_bf[...] = weight_ref[...].astype(jnp.bfloat16)
 
-    def partial_keys(d):
+    def partial_keys(h, d):
         plane = across(d)
         count = PLANE - 1 if d == 0 else PLANE
-        wait_bytes(x_all.at[pl.ds(0, count * rows), :], x_recv_sem.at[plane])
-        part = jnp.dot(x_all[plane_rows(plane), :], w_bf[...],
+        wait_bytes(x_all.at[h, pl.ds(0, count * rows), :], x_recv_sem.at[h, plane])
+        part = jnp.dot(x_all[h, plane_rows(plane), :], w_bf[...],
                        preferred_element_type=jnp.float32)
-        part_f32[d] = part
-        part_bf[d] = part.astype(jnp.bfloat16)
+        part_f32[h, d] = part
+        part_bf[h, d] = part.astype(jnp.bfloat16)
         for e, place in enumerate((last, core)):
-            send(part_bf.at[d, block_rows(place), :], core_recv.at[d, e],
-                 core_send_sem, core_recv_sem.at[d], at(z, core))
-
-    def core_sum(d):
-        wait_bytes(core_recv.at[d], core_recv_sem.at[d])
-        pair_send[d] = (
-            part_f32[d, block_rows(pair), :] + core_recv[d, 0].astype(jnp.float32)
+            send(part_bf.at[h, d, block_rows(place), :], core_recv.at[h, d, e],
+                 core_send_sem.at[h], core_recv_sem.at[h, d], at(z, core))
+
+    def core_sum(h, d):
+        wait_bytes(core_recv.at[h, d], core_recv_sem.at[h, d])
+        pair_send[h, d] = (
+            part_f32[h, d, block_rows(pair), :] + core_recv[h, d, 0].astype(jnp.float32)
         ).astype(jnp.bfloat16)
-        send(pair_send.at[d], pair_recv.at[d], pair_send_sem, pair_recv_sem.at[d],
+        send(pair_send.at[h, d], pair_recv.at[h, d], pair_send_sem.at[h], pair_recv_sem.at[h, d],
              at(z, pair))
 
-    def plane_sum(d):
-        summed = part_f32[d, block_rows(q), :] + core_recv[d, 1].astype(jnp.float32)
-        wait_bytes(pair_recv.at[d], pair_recv_sem.at[d])
-        summed += pair_recv[d].astype(jnp.float32)
+    def plane_sum(h, d):
+        summed = part_f32[h, d, block_rows(q), :] + core_recv[h, d, 1].astype(jnp.float32)
+        wait_bytes(pair_recv.at[h, d], pair_recv_sem.at[h, d])
+        summed += pair_recv[h, d].astype(jnp.float32)
         if d == 0:
-            keys_acc[...] = summed
+            keys_acc[h] = summed
         else:
-            keys_send[d - 1] = summed.astype(jnp.bfloat16)
-            send(keys_send.at[d - 1], keys_recv.at[d - 1], keys_send_sem,
-                 keys_recv_sem, at(across(d), q))
-
-    turns = [0, *order]
-    for step in range(planes + 2):
-        if step < planes:
-            partial_keys(turns[step])
-        if 1 <= step <= planes:
-            core_sum(turns[step - 1])
-        if step >= 2:
-            plane_sum(turns[step - 2])
-
+            keys_send[h, d - 1] = summed.astype(jnp.bfloat16)
+            send(keys_send.at[h, d - 1], keys_recv.at[h, d - 1], keys_send_sem.at[h],
+                 keys_recv_sem.at[h], at(across(d), q))
+
+
+    def pass_on(h, index, target):
+        block = dproj_all.at[h, block_rows(index), :]
+        send(block, block, dproj_send_sem.at[h], dproj_recv_sem.at[h, index], target)
+
+    def arrived(h, index):
+        wait_bytes(dproj_all.at[h, block_rows(index), :], dproj_recv_sem.at[h, index])
+
+    def from_plane(h, d):
+        index = at(across(d), q)
+        arrived(h, index)
+        pass_on(h, index, at(z, pair))
+        pass_on(h, index, at(z, core))
+
+    def from_pair(h, d):
+        index = at(across(d), pair)
+        arrived(h, index)
+        pass_on(h, index, at(z, core))
+
+    def add_plane(h, d):
+        plane = across(d)
+        arrived(h, at(plane, core))
+        arrived(h, at(plane, last))
+        product = lax.dot_general(
+            x_all[h, plane_rows(plane), :], dproj_all[h, plane_rows(plane), :],
+            (((0,), (0,)), ((), ())), preferred_element_type=jnp.float32,
+        )
+        if h == 0 and d == 0:
+            grad_acc[...] = product
+        else:
+            grad_acc[...] += product
+
+    def sum_keys(h):
+        turns = [0, *order]
+        for step in range(planes + 2):
+            if step < planes:
+                partial_keys(h, turns[step])
+            if 1 <= step <= planes:
+                core_sum(h, turns[step - 1])
+            if step >= 2:
+                plane_sum(h, turns[step - 2])
+
+    def start_gather(h):
+        wait_bytes(keys_recv.at[h], keys_recv_sem.at[h])
+        keys = keys_acc[h]
+        for d in range(planes - 1):
+            keys += keys_recv[h, d].astype(jnp.float32)
+        dproj_all[h, block_rows(me), :] = head_backward(
+            keys * factor, cot_ref[h * rows:(h + 1) * rows, :].astype(jnp.float32)
+        )
+
+        for d in order:
+            pass_on(h, me, at(across(d), q))
+        pass_on(h, me, at(z, pair))
+        pass_on(h, me, at(z, core))
+
+    def forward(h):
+        from_pair(h, 0)
+        for d in order:
+            from_plane(h, d)
+        for d in order:
+            from_pair(h, d)
+
+    def add_products(h):
+        for d in (0, *order):
+            add_plane(h, d)
+
+    sum_keys(0)
+    start_gather(0)
+    for h in range(1, HALVES):
+        sum_keys(h)
+        forward(h - 1)
+        start_gather(h)
+        add_products(h - 1)
     wait_bytes(delta_recv, delta_recv_sem)
     outer = delta_buf[...]
     for i in range(n_rep - 1):
         outer += delta_recv[i]
     outer_out[...] = outer
 
-    wait_bytes(keys_recv, keys_recv_sem)
-    keys = keys_acc[...]
-    for d in range(planes - 1):
-        keys += keys_recv[d].astype(jnp.float32)
-    dproj_all[block_rows(me), :] = head_backward(
-        keys * factor, cot_ref[...].astype(jnp.float32)
-    )
-
-
-    def pass_on(index, target):
-        block = dproj_all.at[block_rows(index), :]
-        send(block, block, dproj_send_sem, dproj_recv_sem.at[index], target)
-
-    def arrived(index):
-        wait_bytes(dproj_all.at[block_rows(index), :], dproj_recv_sem.at[index])
-
-    for d in range(1, planes):
-        pass_on(me, at(across(d), q))
-    pass_on(me, at(z, pair))
-    pass_on(me, at(z, core))
-
-    def from_plane(d):
-        index = at(across(d), q)
-        arrived(index)
-        pass_on(index, at(z, pair))
-        pass_on(index, at(z, core))
-
-    def from_pair(d):
-        index = at(across(d), pair)
-        arrived(index)
-        pass_on(index, at(z, core))
-
-    def add_plane(d):
-        plane = across(d)
-        arrived(at(plane, core))
-        arrived(at(plane, last))
-        product = lax.dot_general(
-            x_all[plane_rows(plane), :], dproj_all[plane_rows(plane), :],
-            (((0,), (0,)), ((), ())), preferred_element_type=jnp.float32,
-        )
-        if d == 0:
-            grad_acc[...] = product
-        else:
-            grad_acc[...] += product
-
-    for d in range(1, planes + 2):
-        if d < planes:
-            from_plane(d)
-        if d - 1 < planes:
-            from_pair(d - 1)
-        if d >= 2:
-            add_plane(d - 2)
+    forward(HALVES - 1)
+    add_products(HALVES - 1)
 
     grad = grad_acc[...] * factor
     ones = jnp.ones((8, grad.shape[1]), jnp.float32)
@@ -246,11 +265,12 @@
              lax.rem(me + i, n))
     grad_out[...] = grad
 
-    wait_bytes(normed_buf.at[pl.ds(0, n - 1)], x_send_sem)
-    wait_bytes(core_recv, core_send_sem)
-    wait_bytes(pair_recv, pair_send_sem)
-    wait_bytes(keys_send, keys_send_sem)
-    wait_bytes(dproj_all.at[pl.ds(0, (n - 1) * rows), :], dproj_send_sem)
+    for h in range(HALVES):
+        wait_bytes(normed_buf.at[h, pl.ds(0, n - 1)], x_send_sem.at[h])
+        wait_bytes(core_recv.at[h], core_send_sem.at[h])
+        wait_bytes(pair_recv.at[h], pair_send_sem.at[h])
+        wait_bytes(keys_send.at[h], keys_send_sem.at[h])
+        wait_bytes(dproj_all.at[h, pl.ds(0, (n - 1) * rows), :], dproj_send_sem.at[h])
     wait_bytes(delta_recv, delta_send_sem)
     wait_bytes(gain_buf.at[pl.ds(0, n - 1)], gain_recv_sem)
     for j in range(n):
@@ -261,7 +281,8 @@
 def body(tokens, cotangent, gain, local_weight, stale_weight, global_weight, momentum):
     n = lax.axis_size("fsdp")
     n_rep = lax.axis_size("replica")
-    rows, width = tokens.shape
+    width = tokens.shape[1]
+    rows = tokens.shape[0] // HALVES
     feats, units = global_weight.shape
     planes = n // PLANE
     factor = width ** (-0.5)
@@ -282,27 +303,27 @@
             pltpu.VMEM((feats, units), f32),
             pltpu.VMEM((feats, units), f32),
             pltpu.VMEM((feats, units), f32),
-            pltpu.VMEM((n, rows, feats), bf16),
-            pltpu.VMEM((n * rows, feats), bf16),
+            pltpu.VMEM((HALVES, n, rows, feats), bf16),
+            pltpu.VMEM((HALVES, n * rows, feats), bf16),
             pltpu.VMEM((feats, units), bf16),
-            pltpu.VMEM((planes, PLANE * rows, units), f32),
-            pltpu.VMEM((planes, PLANE * rows, units), bf16),
-            pltpu.VMEM((planes, 2, rows, units), bf16),
-            pltpu.VMEM((planes, rows, units), bf16),
-            pltpu.VMEM((planes, rows, units), bf16),
-            pltpu.VMEM((planes - 1, rows, units), bf16),
-            pltpu.VMEM((planes - 1, rows, units), bf16),
-            pltpu.VMEM((rows, units), f32),
-            pltpu.VMEM((n * rows, units), bf16),
+            pltpu.VMEM((HALVES, planes, PLANE * rows, units), f32),
+            pltpu.VMEM((HALVES, planes, PLANE * rows, units), bf16),
+            pltpu.VMEM((HALVES, planes, 2, rows, units), bf16),
+            pltpu.VMEM((HALVES, planes, rows, units), bf16),
+            pltpu.VMEM((HALVES, planes, rows, units), bf16),
+            pltpu.VMEM((HALVES, planes - 1, rows, units), bf16),
+            pltpu.VMEM((HALVES, planes - 1, rows, units), bf16),
+            pltpu.VMEM((HALVES, rows, units), f32),
+            pltpu.VMEM((HALVES, n * rows, units), bf16),
             pltpu.VMEM((feats, units), f32),
             pltpu.VMEM((feats, units), f32),
             pltpu.VMEM((n_rep - 1, feats, units), f32),
             pltpu.VMEM((n, 1, feats), f32),
-            dma, dma((planes,)),
-            dma, dma((planes,)),
-            dma, dma((planes,)),
-            dma, dma,
-            dma, dma((n,)),
+            dma((HALVES,)), dma((HALVES, planes)),
+            dma((HALVES,)), dma((HALVES, planes)),
+            dma((HALVES,)), dma((HALVES, planes)),
+            dma((HALVES,)), dma((HALVES,)),
+            dma((HALVES,)), dma((HALVES, n)),
             dma, dma,
             dma, dma,
             dma((3,)),

time: 105 us -> 99.7 us (0.950)
  Pallas kernels: 99.5 us -> 94.6 us
    pallas_call x1, Pallas kernels: 99.5 us -> 94.6 us  [body(): pl.pallas_call(functools.partial(kernel, n, n_rep, factor), out_shape=(ja...]
where the time goes in v3:
time: 99.7 us; the launch traced here: 99.6 us
  Pallas kernels  94.6 us (95%)
  other arithmetic  3.63 us (4%)
    pallas_call x1, Pallas kernels, body(): pl.pallas_call(functools.partial(kernel, n, n_rep, factor), out_shape=(ja...  94.6 us
    broadcast_in_dim x1, other arithmetic, body(): return (local_new[None], gain_new, global_new, momentum_new)  3.63 us

profile of v3, /device:TPU:0, one launch (start us, length us, event | category | flops | bytes accessed | tf_op | source)
XLA Modules:
  0.0 99.6 jit_solution(11522626360448934972)
XLA Ops:
  0.6 0.0 copy-start
  0.6 0.0 copy-start.1
  0.7 0.0 copy-start.2
  0.7 94.6 %diloco_step.1 = (f32[512,512]{1,0:T(8,128)}, f32[1,8192]{1,0:T(1,128)}, f32[512,512]{1,0:T(8,128)}) custom-call(bf16[128,8192]{1,0:T(8,128)(2,1)} %tok_ref.1, bf16[128,512]{1,0:T(8,128)(2,1)} %cot_ref.1, f32[1,8192]{1,0:T(1,128)} %gain_ref.1, f32[512,512]{1,0:T(8,128)} %bitcast.5, f32[512,512]{1,0:T(8,128)} %bitcast.6, f32[512,512]{1,0:T(8,128)} %global_hbm.1), custom_call_target="tpu_custom_call" | custom-call | tf_op jit(solution)/shard_map/diloco_step/pallas_call | solution.py:293
  95.3 0.0 copy-done
  95.3 0.0 copy-done.1
  95.3 0.0 copy-done.2
  95.3 0.0 copy-start.3
  95.3 3.6 %multiply_bitcast_fusion = (f32[1,512,512]{2,1,0:T(8,128)}, f32[512,512]{1,0:T(8,128)}, f32[512,512]{1,0:T(8,128)}) fusion(f32[512,512]{1,0:T(8,128)} %get-tuple-element.7, f32[1,512,512]{2,1,0:T(8,128)S(1)} %copy-done, f32[512,512]{1,0:T(8,128)S(1)} %copy-done.1, f32[512,512]{1,0:T(8,128)} %get-tuple-element.8, f32[512,512]{1,0:T(8,128)S(1)} %copy-done.2), kind=kLoop, calls=%fused_computation | loop fusion | flops 2883584 | bytes 8388608 | tf_op jit(solution)/shard_map/broadcast_in_dim | solution.py:341
  98.9 0.0 copy-done.3
  98.9 0.6 copy.12
Async XLA Ops:
  0.6 94.6 %copy-start = (f32[1,512,512]{2,1,0:T(8,128)S(1)}, f32[1,512,512]{2,1,0:T(8,128)}, u32[]{:S(2)}) copy-start(f32[1,512,512]{2,1,0:T(8,128)} %param.10) | copy-start | bytes 3145732
  0.6 94.6 %copy-start.1 = (f32[512,512]{1,0:T(8,128)S(1)}, f32[512,512]{1,0:T(8,128)}, u32[]{:S(2)}) copy-start(f32[512,512]{1,0:T(8,128)} %global_hbm.1) | copy-start | bytes 3145732
  0.7 94.6 %copy-start.2 = (f32[512,512]{1,0:T(8,128)S(1)}, f32[512,512]{1,0:T(8,128)}, u32[]{:S(2)}) copy-start(f32[512,512]{1,0:T(8,128)} %param.13) | copy-start | bytes 3145732
  95.3 3.6 %copy-start.3 = (f32[1,8192]{1,0:T(1,128)S(1)}, f32[1,8192]{1,0:T(1,128)}, u32[]{:S(2)}) copy-start(f32[1,8192]{1,0:T(1,128)} %get-tuple-element.18) | copy-start | bytes 98308
